TPU v7x, 32 devices: a whole 2x2x4 slice. The times are simulated.
32 devices in a mesh: members: 2 (over y), lon: 4 (over z), lat: 2 (over x), lev: 2 (over core).
Axes of the slice: x: 2, y: 2, z: 4, core: 2. Of those that a mesh axis runs over, the one named last changes fastest.
Arguments:
- ash_density_field: float32 [12, 4, 256, 512], P('members', 'lev', 'lat', 'lon'), parts along dimension 0, may hold values from 0.05 to 5
- face_transport_numbers: float32 [2, 4, 256, 512], P(None, 'lev', 'lat', 'lon'), may hold values from -0.15 to 0.15
- spreading_number: float32 [6, 4], replicated, may hold values from 0.01 to 0.03
- particle_fall_category: int32 [6], replicated, may hold values from 0 to 3
- crater_parallel_position: int32 [8], P('members'), parts along dimension 0, may hold values from 0 to 255
- crater_meridian_position: int32 [8], P('members'), parts along dimension 0, may hold values from 0 to 511
- crater_release_altitude: int32 [8], P('members'), parts along dimension 0, may hold values from 0 to 3
- eruption_source_amount: float32 [8, 6], P('members'), parts along dimension 0, may hold values from 0.5 to 4
- optical_depth_factor: float32 [8, 6], replicated, may hold values from 0.005 to 0.05
- spectral_radiance_share: float32 [8], replicated, may hold values from 0.5 to 2
- atmosphere_warmth: float32 [4, 256, 512], P('lev', 'lat', 'lon'), may hold values from 200 to 290
- ground_warmth_kelvin: float32 [256, 512], P('lat', 'lon'), may hold values from 250 to 310
Outputs:
- settled: float32 [12, 4, 256, 512], P('members', 'lev', 'lat', 'lon'), parts along dimension 0
- upwelling: float32 [16, 4, 256, 512], P('members', 'lev', 'lat', 'lon'), parts along dimension 0
There are 2 independent parts, one for each index of `members`. A program takes and returns all parts, laid end to end along the dimension named above; an argument that names none is the same for every part. Nothing has to cross between parts.
Inputs may be any that keep to these rules, and one draw needn't show every extreme that they name: `particle_fall_category`: a settling class for each grain size. `crater_parallel_position`: vents may share a cell.
All inputs are finite; a program needn't handle non-finite values.
Results may differ from a plain program's by a relative error of at most 0.0001.
Values sent between devices are 32-bit elements; how exact they have to be, the bound alone decides.
A program may use at most 64 MiB of HBM per device.

v0:
```python
import jax
import jax.numpy as jnp
from jax import lax
from jax.sharding import PartitionSpec as P

STEPS = 2


def shifted(block, axis, distance):
    devices = range(lax.axis_size(axis))
    route = [((i - distance) % len(devices), i) for i in devices]
    return lax.ppermute(block, axis, route)


def shifted_2(shard, axis, by):
    size = lax.axis_size(axis)
    pairs = [(i, i + by) for i in range(size) if 0 <= i + by < size]
    return lax.ppermute(shard, axis, pairs)


def with_halo(cells, sides, width, closed):
    for axis, dim in sides:
        count = lax.axis_size(axis)
        ends = count if closed else count - 1
        head = lax.slice_in_dim(cells, 0, width, axis=dim)
        tail = lax.slice_in_dim(cells, cells.shape[dim] - width, cells.shape[dim], axis=dim)
        cells = jnp.concatenate(
            [
                lax.ppermute(tail, axis, [(i, (i + 1) % count) for i in range(ends)]),
                cells,
                lax.ppermute(head, axis, [((i + 1) % count, i) for i in range(ends)]),
            ],
            axis=dim,
        )
    return cells


def prefix(value, axis, join, neutral):
    count, mine = (lax.axis_size(axis), lax.axis_index(axis))
    pieces = jax.tree.map(lambda part: lax.all_gather(part, axis), value)
    subtotal = jax.tree.map(
        lambda part, zero: jnp.full_like(part, 0) + jnp.asarray(zero, part.dtype), value, neutral
    )

    def turn(position, subtotal):
        longer = join(subtotal, jax.tree.map(lambda part: part[position], pieces))
        return jax.tree.map(lambda new, old: jnp.where(position < mine, new, old), longer, subtotal)

    return lax.fori_loop(0, count - 1, turn, subtotal)


def update(
    density, east_cell, west_cell, north_cell, south_cell, above_cell, winds, mixing, settle
):
    u_east, u_west, v_north, v_south = winds
    flux_east = jnp.maximum(u_east, 0.0) * density + jnp.minimum(u_east, 0.0) * east_cell
    flux_west = jnp.maximum(u_west, 0.0) * west_cell + jnp.minimum(u_west, 0.0) * density
    flux_north = jnp.maximum(v_north, 0.0) * density + jnp.minimum(v_north, 0.0) * north_cell
    flux_south = jnp.maximum(v_south, 0.0) * south_cell + jnp.minimum(v_south, 0.0) * density
    laplace = east_cell + west_cell + north_cell + south_cell - 4.0 * density
    return (
        density
        - (flux_east - flux_west)
        - (flux_north - flux_south)
        + mixing * laplace
        + settle * (above_cell - density)
    )


def combine_slabs(earlier, later):
    return (earlier[0] * later[0], earlier[1] * later[0] + later[1])


def vent_field(
    eruption_source_amount,
    crater_release_altitude,
    crater_parallel_position,
    crater_meridian_position,
    level_ids,
    row_ids,
    col_ids,
):
    vent_count, grain_count = eruption_source_amount.shape
    level_hot = (crater_release_altitude[:, None] == level_ids[None, :]).astype(jnp.float32)
    lat_hot = (crater_parallel_position[:, None] == row_ids[None, :]).astype(jnp.float32)
    lon_hot = (crater_meridian_position[:, None] == col_ids[None, :]).astype(jnp.float32)
    left_side = (eruption_source_amount[:, :, None] * level_hot[:, None, :]).reshape(
        vent_count, grain_count * level_ids.shape[0]
    )
    right_side = (lat_hot[:, :, None] * lon_hot[:, None, :]).reshape(
        vent_count, row_ids.shape[0] * col_ids.shape[0]
    )
    product = jnp.dot(left_side.T, right_side, precision=lax.Precision.HIGHEST)
    return product.reshape(grain_count, level_ids.shape[0], row_ids.shape[0], col_ids.shape[0])


def per_device(
    ash_density_field,
    face_transport_numbers,
    spreading_number,
    particle_fall_category,
    crater_parallel_position,
    crater_meridian_position,
    crater_release_altitude,
    eruption_source_amount,
    optical_depth_factor,
    spectral_radiance_share,
    atmosphere_warmth,
    ground_warmth_kelvin,
):
    grain_count, slab_levels, lat_rows, lon_cols = ash_density_field.shape
    band_count = optical_depth_factor.shape[0]
    lev_start = lax.axis_index("lev") * slab_levels
    lat_start = lax.axis_index("lat") * lat_rows
    lon_start = lax.axis_index("lon") * lon_cols
    is_south = lax.axis_index("lat") == 0
    is_north = lax.axis_index("lat") == lax.axis_size("lat") - 1
    half_cycle = lax.axis_size("lon") // 2
    fall_rate = (0.04 * (1.0 + particle_fall_category.astype(jnp.float32)))[:, None, None, None]
    mixing = lax.dynamic_slice_in_dim(spreading_number, lev_start, slab_levels, 1)[:, :, None, None]
    u_east = face_transport_numbers[0]
    row_ids = jnp.arange(lat_rows, dtype=jnp.int32)[None, :, None]
    v_north = jnp.where(is_north & (row_ids == lat_rows - 1), 0.0, face_transport_numbers[1])
    west_edge = shifted(u_east[:, :, -1:], "lon", 1)
    u_west = jnp.concatenate([west_edge, u_east[:, :, :-1]], axis=2)
    south_edge = shifted_2(v_north[:, -1:, :], "lat", 1)
    v_south = jnp.concatenate([south_edge, v_north[:, :-1, :]], axis=1)
    winds = (u_east, u_west, v_north, v_south)
    inject = vent_field(
        eruption_source_amount,
        crater_release_altitude,
        crater_parallel_position,
        crater_meridian_position,
        lev_start + jnp.arange(slab_levels, dtype=jnp.int32),
        lat_start + jnp.arange(lat_rows, dtype=jnp.int32),
        lon_start + jnp.arange(lon_cols, dtype=jnp.int32),
    )
    density = ash_density_field
    for step_index in range(STEPS):
        lon_ext = with_halo(density, (("lon", 3),), 1, True)
        west_cell = lon_ext[:, :, :, :-2]
        east_cell = lon_ext[:, :, :, 2:]
        lat_ext = with_halo(density, (("lat", 2),), 1, False)
        south_cell = lat_ext[:, :, :-2, :]
        north_cell = lat_ext[:, :, 2:, :]
        partner = shifted(jnp.stack([density[:, :, 0], density[:, :, -1]]), "lon", half_cycle)
        south_cell = south_cell.at[:, :, 0].set(
            jnp.where(is_south, partner[0], south_cell[:, :, 0])
        )
        north_cell = north_cell.at[:, :, -1].set(
            jnp.where(is_north, partner[1], north_cell[:, :, -1])
        )
        above_rim = shifted_2(density[:, :1], "lev", -1)
        above_cell = jnp.concatenate([density[:, 1:], above_rim], axis=1)
        density = (
            update(
                density,
                east_cell,
                west_cell,
                north_cell,
                south_cell,
                above_cell,
                winds,
                mixing,
                fall_rate,
            )
            + inject
        )
    scale = spectral_radiance_share[:, None, None]
    proportion_quotient = ground_warmth_kelvin / 250.0
    squared = proportion_quotient * proportion_quotient
    surface_rad = scale * (squared * squared)
    transmits = []
    emits = []
    slab_trans = jnp.ones((band_count, lat_rows, lon_cols), jnp.float32)
    slab_emit = jnp.zeros((band_count, lat_rows, lon_cols), jnp.float32)
    for altitude_tier_position in range(slab_levels):
        optical = jnp.dot(
            optical_depth_factor,
            density[:, altitude_tier_position].reshape(grain_count, lat_rows * lon_cols),
            precision=lax.Precision.HIGHEST,
        ).reshape(band_count, lat_rows, lon_cols)
        transmit = jnp.exp(-optical)
        proportion_quotient = atmosphere_warmth[altitude_tier_position] / 250.0
        squared = proportion_quotient * proportion_quotient
        emitted = scale * (squared * squared)
        slab_emit = slab_emit * transmit + emitted * (1.0 - transmit)
        slab_trans = slab_trans * transmit
        transmits.append(transmit)
        emits.append(emitted)
    prefix_trans, prefix_emit = prefix(
        (slab_trans, slab_emit),
        "lev",
        combine_slabs,
        (jnp.ones_like(slab_trans), jnp.zeros_like(slab_emit)),
    )
    radiance = prefix_emit + prefix_trans * surface_rad
    layers = []
    for altitude_tier_position in range(slab_levels):
        radiance = radiance * transmits[altitude_tier_position] + emits[altitude_tier_position] * (
            1.0 - transmits[altitude_tier_position]
        )
        layers.append(radiance)
    return (density, jnp.stack(layers, axis=1))


def solution(mesh):
    placed = (
        P("members", "lev", "lat", "lon"),
        P(None, "lev", "lat", "lon"),
        P(),
        P(),
        P("members"),
        P("members"),
        P("members"),
        P("members", None),
        P(),
        P(),
        P("lev", "lat", "lon"),
        P("lat", "lon"),
    )
    return jax.shard_map(
        per_device,
        mesh=mesh,
        in_specs=placed,
        out_specs=(P("members", "lev", "lat", "lon"), P("members", "lev", "lat", "lon")),
        check_vma=False,
    )
```

profile of v0, /device:TPU:0, one launch (start us, length us, event | category | flops | bytes accessed | tf_op | source)
XLA Modules:
  0.0 120.3 jit_solution(4938714281929387446)
XLA Ops:
  7.2 1.7 %copy.153 = f32[6,2,128,128]{3,0,2,1:T(8,128)S(1)} copy(f32[6,2,128,128]{3,2,1,0:T(8,128)} %param.20) | data formatting | bytes 1572864 | tf_op args[0]
  11.4 6.0 %collective-permute-start.6 = (f32[6,2,1,128]{3,0,1,2:T(8,128)}, f32[6,2,1,128]{3,0,1,2:T(8,128)}, u32[]{:S(2)}, u32[]{:S(2)}) collective-permute-start(f32[6,2,1,128]{3,0,1,2:T(8,128)} %copy.216), channel_id=1, source_target_pairs={{0,2},{1,3},{4,6},{5,7},{8,10},{9,11},{12,14},{13,15},{16,18},{17,... | collective-permute-start | bytes 18440 | tf_op jit(solution)/shard_map/ppermute | solution.py:29
  18.7 3.7 %collective-permute-start.4 = (f32[2,6,2,128]{3,1,2,0:T(8,128)}, f32[2,6,2,128]{3,1,2,0:T(8,128)}, u32[]{:S(2)}, u32[]{:S(2)}) collective-permute-start(f32[2,6,2,128]{3,1,2,0:T(8,128)} %pad_maximum_fusion.11), channel_id=1, source_target_pairs={{8,0},{12,4},{0,8},{4,12},{9,1},{13,5},{1,9},{5,13},{10,2},{14,6},... | collective-permute-start | bytes 36872 | tf_op jit(solution)/shard_map/ppermute | solution.py:12
  24.0 1.6 %collective-permute-start.1 = (f32[2,128,1]{2,1,0:T(8,128)}, f32[2,128,1]{2,1,0:T(8,128)}, u32[]{:S(2)}, u32[]{:S(2)}) collective-permute-start(f32[2,128,1]{2,1,0:T(8,128)} %slice.258), channel_id=1, source_target_pairs={{12,0},{0,4},{4,8},{8,12},{13,1},{1,5},{5,9},{9,13},{14,2},{2,6},{... | collective-permute-start | bytes 3080 | tf_op jit(solution)/shard_map/ppermute | solution.py:12
  26.2 1.8 %collective-permute-start.5 = (f32[2,1,128]{2,1,0:T(1,128)}, f32[2,1,128]{2,1,0:T(1,128)}, u32[]{:S(2)}, u32[]{:S(2)}) collective-permute-start(f32[2,1,128]{2,1,0:T(1,128)} %slice.262), channel_id=1, source_target_pairs={{0,2},{1,3},{4,6},{5,7},{8,10},{9,11},{12,14},{13,15},{16,18},{17,... | collective-permute-start | bytes 3080 | tf_op jit(solution)/shard_map/ppermute | solution.py:18
  29.1 1.4 %fusion.34 = (f32[6,2,128,1]{3,2,1,0:T(8,128)}, f32[6,2,128,1]{3,2,1,0:T(8,128)}) fusion(f32[6,2,128,128]{3,2,1,0:T(8,128)S(1)} %copy-done.1), kind=kLoop, calls=%fused_computation.90 | loop fusion | bytes 24576 | tf_op jit(solution)/shard_map/slice | solution.py:25
  35.9 2.0 %copy.195 = f32[6,2,128,1]{2,1,3,0:T(2,128)} copy(f32[6,2,128,1]{3,2,1,0:T(8,128)} %get-tuple-element.99) | data formatting | bytes 12288
  39.5 1.7 %broadcast_maximum_fusion = (f32[2,128,128]{2,1,0:T(8,128)}, f32[2,128,128]{2,1,0:T(8,128)}) fusion(f32[2,128,127]{2,1,0:T(8,128)S(1)} %bitcast.134, f32[2,128,1]{2,1,0:T(8,128)} %collective-permute-done.1), kind=kLoop, calls=%fused_computation.51 | loop fusion | flops 98304 | bytes 393216 | tf_op jit(solution)/shard_map/max | solution.py:57
  41.2 2.3 %collective-permute-start = (f32[6,2,128,1]{2,1,3,0:T(2,128)S(1)}, f32[6,2,128,1]{2,1,3,0:T(2,128)S(1)}, u32[]{:S(2)}, u32[]{:S(2)}) collective-permute-start(f32[6,2,128,1]{2,1,3,0:T(2,128)S(1)} %copy-done.9), channel_id=1, source_target_pairs={{4,0},{8,4},{12,8},{0,12},{5,1},{9,5},{13,9},{1,13},{6,2},{10,6},{... | collective-permute-start | bytes 18440 | tf_op jit(solution)/shard_map/ppermute | solution.py:31
  43.5 1.4 %fusion.16 = (f32[2,128,128]{2,1,0:T(8,128)}, f32[2,128,128]{2,1,0:T(8,128)}) fusion(f32[2,127,128]{2,1,0:T(8,128)S(1)} %bitcast.135, f32[2,1,128]{2,1,0:T(1,128)} %collective-permute-done.5), kind=kLoop, calls=%fused_computation.46 | loop fusion | flops 98304 | bytes 393216 | tf_op jit(solution)/shard_map/max | solution.py:59
  44.9 2.2 %pad_maximum_fusion.5 = (f32[6,2,128,128]{3,0,2,1:T(8,128)}, f32[6,2,128,128]{3,0,2,1:T(8,128)}) fusion(f32[6,2,1,128]{3,0,2,1:T(8,128)} %collective-permute-done.3, f32[6,2,128,128]{3,0,2,1:T(8,128)S(1)} %copy.153, f32[6,2,1,128]{3,0,2,1:T(8,128)} %bitcast.11), kind=kLoop, calls=%fused_computation.9 | loop fusion | flops 393216 | bytes 2371584 | tf_op jit(solution)/shard_map/concatenate | solution.py:27
  47.0 1.3 %copy.148 = f32[6,2,128,1]{3,0,2,1:T(8,128)} copy(f32[6,2,128,1]{2,1,3,0:T(2,128)S(1)} %collective-permute-done) | data formatting | bytes 12288 | tf_op jit(solution)/shard_map/ppermute | solution.py:31
  48.4 1.9 %collective-permute-done.2 = f32[6,2,128,1]{2,1,3,0:T(2,128)S(1)} collective-permute-done((f32[6,2,128,1]{2,1,3,0:T(2,128)S(1)}, f32[6,2,128,1]{2,1,3,0:T(2,128)S(1)}, u32[]{:S(2)}, u32[]{:S(2)}) %collective-permute-start.2) | collective-permute-done | bytes 6176 | tf_op jit(solution)/shard_map/ppermute | solution.py:29
  50.3 1.4 %copy.150 = f32[6,2,128,1]{3,0,2,1:T(8,128)} copy(f32[6,2,128,1]{2,1,3,0:T(2,128)S(1)} %collective-permute-done.2) | data formatting | bytes 12288 | tf_op jit(solution)/shard_map/ppermute | solution.py:29
  54.5 3.4 %fusion.4 = f32[6,2,128,128]{3,0,2,1:T(8,128)S(1)} fusion(f32[6,2,128,128]{3,0,2,1:T(8,128)S(1)} %fusion.13, f32[6,2,128,128]{3,0,2,1:T(8,128)S(1)} %copy.153, f32[6,1,128,128]{3,0,2,1:T(8,128)} %copy-done.6, f32[6,1,128,128]{3,0,2,1:T(8,128)} %get-tuple-element.97, f32[6,2,128,128]{3,0,2,1:T(8,128)} %get-tuple-element.117, ...), kind=kLoop, calls=%fused_computation.15 | loop fusion | flops 5898240 | bytes 5779528 | tf_op jit(solution)/shard_map/add | solution.py:156
  62.1 5.1 %collective-permute-start.12 = (f32[6,2,1,128]{3,0,1,2:T(8,128)}, f32[6,2,1,128]{3,0,1,2:T(8,128)}, u32[]{:S(2)}, u32[]{:S(2)}) collective-permute-start(f32[6,2,1,128]{3,0,1,2:T(8,128)} %get-tuple-element.90), channel_id=1, source_target_pairs={{0,2},{1,3},{4,6},{5,7},{8,10},{9,11},{12,14},{13,15},{16,18},{17,... | collective-permute-start | bytes 18440 | tf_op jit(solution)/shard_map/ppermute | solution.py:29
  69.2 2.1 %copy.170 = f32[6,2,128,1]{2,1,3,0:T(2,128)} copy(f32[6,2,128,1]{3,0,2,1:T(8,128)} %get-tuple-element.83) | data formatting | bytes 12288 | tf_op jit(solution)/shard_map/slice | solution.py:25
  71.2 1.9 %collective-permute-start.8 = (f32[6,2,128,1]{2,1,3,0:T(2,128)}, f32[6,2,128,1]{2,1,3,0:T(2,128)}, u32[]{:S(2)}, u32[]{:S(2)}) collective-permute-start(f32[6,2,128,1]{2,1,3,0:T(2,128)} %copy.170), channel_id=1, source_target_pairs={{4,0},{8,4},{12,8},{0,12},{5,1},{9,5},{13,9},{1,13},{6,2},{10,6},{... | collective-permute-start | bytes 18440 | tf_op jit(solution)/shard_map/ppermute | solution.py:31
  74.6 2.2 %pad_maximum_fusion.1 = (f32[6,2,128,128]{3,0,2,1:T(8,128)}, f32[6,2,128,128]{3,0,2,1:T(8,128)}) fusion(f32[6,2,1,128]{3,0,2,1:T(8,128)S(1)} %bitcast.137, f32[6,2,128,128]{3,0,2,1:T(8,128)S(1)} %fusion.4, f32[6,2,1,128]{3,0,2,1:T(8,128)} %bitcast.24), kind=kLoop, calls=%fused_computation.5 | loop fusion | flops 393216 | bytes 2371584 | tf_op jit(solution)/shard_map/concatenate | solution.py:27
  76.8 2.1 %copy.171 = f32[6,2,128,1]{3,0,2,1:T(8,128)} copy(f32[6,2,128,1]{2,1,3,0:T(2,128)} %collective-permute-done.8) | data formatting | bytes 12288 | tf_op jit(solution)/shard_map/ppermute | solution.py:31
  83.0 3.4 %fusion.7 = f32[6,2,128,128]{3,0,2,1:T(8,128)S(1)} fusion(f32[6,2,128,128]{3,0,2,1:T(8,128)S(1)} %fusion.13, f32[6,2,128,128]{3,0,2,1:T(8,128)S(1)} %fusion.4, f32[6,1,128,128]{3,0,2,1:T(8,128)} %collective-permute-done.13, f32[6,1,128,128]{3,0,2,1:T(8,128)} %get-tuple-element.91, f32[6,2,128,128]{3,0,2,1:T(8,128)} %get-tuple-element.115, ...), kind=kLoop, calls=%fused_computation.19 | loop fusion | flops 5898240 | bytes 5779528 | tf_op jit(solution)/shard_map/add | solution.py:156
  91.5 7.4 %all-gather.3.cloned.1.call-done = f32[2,8,128,128]{3,2,1,0:T(8,128)} async-done(((f32[1,8,128,128]{3,2,1,0:T(8,128)}), f32[2,8,128,128]{3,2,1,0:T(8,128)}) %all-gather.3.cloned.1.call-update) | async-done | bytes 1048592 | tf_op jit(solution)/shard_map/all_gather | solution.py:40
  98.9 11.8 %all-gather.5.cloned.1.call-done = f32[2,8,128,128]{3,2,1,0:T(8,128)} async-done(((f32[1,8,128,128]{3,2,1,0:T(8,128)}), f32[2,8,128,128]{3,2,1,0:T(8,128)}) %all-gather.5.cloned.1.call-update) | async-done | bytes 1048592 | tf_op jit(solution)/shard_map/all_gather | solution.py:40
  110.7 1.6 %multiply_add_fusion = (f32[8,1,128,128]{3,2,0,1:T(8,128)S(1)}, f32[8,1,128,128]{3,2,0,1:T(8,128)S(1)}) fusion(f32[8,1,128,128]{3,0,2,1:T(8,128)S(1)} %bitcast.133, f32[128,128]{1,0:T(8,128)S(1)} %copy-done.5, f32[8]{0:T(128)S(1)} %copy-done.10, f32[128,128]{1,0:T(8,128)S(1)} %copy-done.4, f32[8,1,128,128]{3,0,2,1:T(8,128)S(1)} %bitcast.131, ...), kind=kLoop, calls=%fused_computation.30 | loop fusion | flops 2228224 | bytes 3342369 | tf_op jit(solution)/shard_map/add | solution.py:200
  (102 shorter events, 34.7 us)
Async XLA Ops:
  7.2 79.3 %copy-start = (f32[8,6]{1,0:T(8,128)S(1)}, f32[8,6]{1,0:T(8,128)}, u32[]{:S(2)}) copy-start(f32[8,6]{1,0:T(8,128)} %param.28) | copy-start | bytes 580
  7.2 3.6 %copy-start.1 = (f32[6,2,128,128]{3,2,1,0:T(8,128)S(1)}, f32[6,2,128,128]{3,2,1,0:T(8,128)}, u32[]{:S(2)}) copy-start(f32[6,2,128,128]{3,2,1,0:T(8,128)} %param.20) | copy-start | bytes 2359300
  7.2 91.7 %all-gather.3.cloned.1.call-start = ((), (), s32[]{:S(2)}) async-start(), calls=%async_computation | async-start | bytes 1572864 | tf_op jit(solution)/shard_map/all_gather | solution.py:40
  7.2 15.3 %copy-start.3 = (f32[2,2,128,128]{3,2,1,0:T(8,128)S(1)}, f32[2,2,128,128]{3,2,1,0:T(8,128)}, u32[]{:S(2)}) copy-start(f32[2,2,128,128]{3,2,1,0:T(8,128)} %param.21) | copy-start | bytes 786436
  9.5 35.3 %collective-permute-start.3 = (f32[6,2,1,128]{3,0,2,1:T(8,128)}, f32[6,2,1,128]{3,0,2,1:T(8,128)}, u32[]{:S(2)}, u32[]{:S(2)}) collective-permute-start(f32[6,2,1,128]{3,0,2,1:T(8,128)} %get-tuple-element.95), channel_id=1, source_target_pairs={{2,0},{3,1},{6,4},{7,5},{10,8},{11,9},{14,12},{15,13},{18,16},{19,... | collective-permute-start | bytes 18440 | tf_op jit(solution)/shard_map/ppermute | solution.py:31
  11.4 33.4 %collective-permute-start.6 = (f32[6,2,1,128]{3,0,1,2:T(8,128)}, f32[6,2,1,128]{3,0,1,2:T(8,128)}, u32[]{:S(2)}, u32[]{:S(2)}) collective-permute-start(f32[6,2,1,128]{3,0,1,2:T(8,128)} %copy.216), channel_id=1, source_target_pairs={{0,2},{1,3},{4,6},{5,7},{8,10},{9,11},{12,14},{13,15},{16,18},{17,... | collective-permute-start | bytes 18440 | tf_op jit(solution)/shard_map/ppermute | solution.py:29
  18.7 32.9 %collective-permute-start.4 = (f32[2,6,2,128]{3,1,2,0:T(8,128)}, f32[2,6,2,128]{3,1,2,0:T(8,128)}, u32[]{:S(2)}, u32[]{:S(2)}) collective-permute-start(f32[2,6,2,128]{3,1,2,0:T(8,128)} %pad_maximum_fusion.11), channel_id=1, source_target_pairs={{8,0},{12,4},{0,8},{4,12},{9,1},{13,5},{1,9},{5,13},{10,2},{14,6},... | collective-permute-start | bytes 36872 | tf_op jit(solution)/shard_map/ppermute | solution.py:12
  24.0 14.2 %collective-permute-start.1 = (f32[2,128,1]{2,1,0:T(8,128)}, f32[2,128,1]{2,1,0:T(8,128)}, u32[]{:S(2)}, u32[]{:S(2)}) collective-permute-start(f32[2,128,1]{2,1,0:T(8,128)} %slice.258), channel_id=1, source_target_pairs={{12,0},{0,4},{4,8},{8,12},{13,1},{1,5},{5,9},{9,13},{14,2},{2,6},{... | collective-permute-start | bytes 3080 | tf_op jit(solution)/shard_map/ppermute | solution.py:12
  26.2 15.0 %collective-permute-start.5 = (f32[2,1,128]{2,1,0:T(1,128)}, f32[2,1,128]{2,1,0:T(1,128)}, u32[]{:S(2)}, u32[]{:S(2)}) collective-permute-start(f32[2,1,128]{2,1,0:T(1,128)} %slice.262), channel_id=1, source_target_pairs={{0,2},{1,3},{4,6},{5,7},{8,10},{9,11},{12,14},{13,15},{16,18},{17,... | collective-permute-start | bytes 3080 | tf_op jit(solution)/shard_map/ppermute | solution.py:18
  29.1 4.1 %copy-start.7 = (f32[2,128,128]{2,1,0:T(8,128)S(1)}, f32[2,128,128]{2,1,0:T(8,128)}, u32[]{:S(2)}) copy-start(f32[2,128,128]{2,1,0:T(8,128)} %param.30) | copy-start | bytes 393220
  34.1 3.8 %copy-start.2 = (f32[6,2,128,1]{3,2,1,0:T(8,128)S(1)}, f32[6,2,128,1]{3,2,1,0:T(8,128)}, u32[]{:S(2)}) copy-start(f32[6,2,128,1]{3,2,1,0:T(8,128)} %get-tuple-element.100) | copy-start | bytes 18436
  38.2 14.8 %collective-permute-start.7 = (f32[6,1,128,128]{3,0,2,1:T(8,128)}, f32[6,1,128,128]{3,0,2,1:T(8,128)S(1)}, u32[]{:S(2)}, u32[]{:S(2)}) collective-permute-start(f32[6,1,128,128]{3,0,2,1:T(8,128)} %get-tuple-element.98), channel_id=1, source_target_pairs={{1,0},{3,2},{5,4},{7,6},{9,8},{11,10},{13,12},{15,14},{17,16},{19,... | collective-permute-start | bytes 1179656 | tf_op jit(solution)/shard_map/ppermute | solution.py:18
  39.5 1.7 %copy-start.9 = (f32[6,2,128,1]{2,1,3,0:T(2,128)S(1)}, f32[6,2,128,1]{2,1,3,0:T(2,128)}, u32[]{:S(2)}) copy-start(f32[6,2,128,1]{2,1,3,0:T(2,128)} %copy.195) | copy-start | bytes 18436
  41.2 5.8 %collective-permute-start = (f32[6,2,128,1]{2,1,3,0:T(2,128)S(1)}, f32[6,2,128,1]{2,1,3,0:T(2,128)S(1)}, u32[]{:S(2)}, u32[]{:S(2)}) collective-permute-start(f32[6,2,128,1]{2,1,3,0:T(2,128)S(1)} %copy-done.9), channel_id=1, source_target_pairs={{4,0},{8,4},{12,8},{0,12},{5,1},{9,5},{13,9},{1,13},{6,2},{10,6},{... | collective-permute-start | bytes 18440 | tf_op jit(solution)/shard_map/ppermute | solution.py:31
  44.9 5.4 %collective-permute-start.2 = (f32[6,2,128,1]{2,1,3,0:T(2,128)S(1)}, f32[6,2,128,1]{2,1,3,0:T(2,128)S(1)}, u32[]{:S(2)}, u32[]{:S(2)}) collective-permute-start(f32[6,2,128,1]{2,1,3,0:T(2,128)S(1)} %copy.196), channel_id=1, source_target_pairs={{0,4},{4,8},{8,12},{12,0},{1,5},{5,9},{9,13},{13,1},{2,6},{6,10},{... | collective-permute-start | bytes 18440 | tf_op jit(solution)/shard_map/ppermute | solution.py:29
  60.8 13.2 %collective-permute-start.10 = (f32[6,2,1,128]{3,0,1,2:T(8,128)}, f32[6,2,1,128]{3,0,1,2:T(8,128)S(1)}, u32[]{:S(2)}, u32[]{:S(2)}) collective-permute-start(f32[6,2,1,128]{3,0,1,2:T(8,128)} %get-tuple-element.87), channel_id=1, source_target_pairs={{2,0},{3,1},{6,4},{7,5},{10,8},{11,9},{14,12},{15,13},{18,16},{19,... | collective-permute-start | bytes 18440 | tf_op jit(solution)/shard_map/ppermute | solution.py:31
  62.1 12.5 %collective-permute-start.12 = (f32[6,2,1,128]{3,0,1,2:T(8,128)}, f32[6,2,1,128]{3,0,1,2:T(8,128)}, u32[]{:S(2)}, u32[]{:S(2)}) collective-permute-start(f32[6,2,1,128]{3,0,1,2:T(8,128)} %get-tuple-element.90), channel_id=1, source_target_pairs={{0,2},{1,3},{4,6},{5,7},{8,10},{9,11},{12,14},{13,15},{16,18},{17,... | collective-permute-start | bytes 18440 | tf_op jit(solution)/shard_map/ppermute | solution.py:29
  67.3 15.1 %collective-permute-start.13 = (f32[6,1,128,128]{3,0,2,1:T(8,128)}, f32[6,1,128,128]{3,0,2,1:T(8,128)}, u32[]{:S(2)}, u32[]{:S(2)}) collective-permute-start(f32[6,1,128,128]{3,0,2,1:T(8,128)} %get-tuple-element.92), channel_id=1, source_target_pairs={{1,0},{3,2},{5,4},{7,6},{9,8},{11,10},{13,12},{15,14},{17,16},{19,... | collective-permute-start | bytes 1179656 | tf_op jit(solution)/shard_map/ppermute | solution.py:18
  69.2 11.9 %collective-permute-start.11 = (f32[2,6,2,128]{3,1,2,0:T(8,128)}, f32[2,6,2,128]{3,1,2,0:T(8,128)}, u32[]{:S(2)}, u32[]{:S(2)}) collective-permute-start(f32[2,6,2,128]{3,1,2,0:T(8,128)} %pad_maximum_fusion.12), channel_id=1, source_target_pairs={{8,0},{12,4},{0,8},{4,12},{9,1},{13,5},{1,9},{5,13},{10,2},{14,6},... | collective-permute-start | bytes 36872 | tf_op jit(solution)/shard_map/ppermute | solution.py:12
  71.2 5.6 %collective-permute-start.8 = (f32[6,2,128,1]{2,1,3,0:T(2,128)}, f32[6,2,128,1]{2,1,3,0:T(2,128)}, u32[]{:S(2)}, u32[]{:S(2)}) collective-permute-start(f32[6,2,128,1]{2,1,3,0:T(2,128)} %copy.170), channel_id=1, source_target_pairs={{4,0},{8,4},{12,8},{0,12},{5,1},{9,5},{13,9},{1,13},{6,2},{10,6},{... | collective-permute-start | bytes 18440 | tf_op jit(solution)/shard_map/ppermute | solution.py:31
  74.1 5.6 %collective-permute-start.9 = (f32[6,2,128,1]{2,1,3,0:T(2,128)}, f32[6,2,128,1]{2,1,3,0:T(2,128)S(1)}, u32[]{:S(2)}, u32[]{:S(2)}) collective-permute-start(f32[6,2,128,1]{2,1,3,0:T(2,128)} %copy.172), channel_id=1, source_target_pairs={{0,4},{4,8},{8,12},{12,0},{1,5},{5,9},{9,13},{13,1},{2,6},{6,10},{... | collective-permute-start | bytes 18440 | tf_op jit(solution)/shard_map/ppermute | solution.py:29
  87.1 0.9 copy-start.5
  89.6 21.1 %all-gather.5.cloned.1.call-start = ((), (), s32[]{:S(2)}) async-start(), calls=%async_computation.1 | async-start | bytes 1572864 | tf_op jit(solution)/shard_map/all_gather | solution.py:40
  89.6 0.8 copy-start.8
  (11 other events, 7.7 us)
Sparse Core Ops, SparseCore 0:
  89.7 9.1 all-gather.2
  100.4 10.1 all-gather.4
where the time goes:
time: 121 us; the launch traced here: 120 us
  local copies, waits for them, and re-layouts  28.7 us (24%)
  starting transfers between devices  28.2 us (23%)
  other arithmetic  24.1 us (20%)
  waiting for transfers between devices  22.7 us (19%)
  between operations  14.3 us (12%)
  matrix products  2.28 us (2%)
    all_gather x2, waiting for transfers between devices, prefix(): pieces = jax.tree.map(lambda part: lax.all_gather(part, axis), value)  19.2 us
    unnamed x45, local copies, waits for them, and re-layouts  12.3 us
    ppermute x4, starting transfers between devices, with_halo(): lax.ppermute(tail, axis, [(i, (i + 1) % count) for i in range(ends)])  11.7 us
    add x2, other arithmetic, per_device(): update(density, east_cell, west_cell, north_cell, south_cell, above_cell,...  6.8 us
    ppermute x4, starting transfers between devices, with_halo(): lax.ppermute(head, axis, [((i + 1) % count, i) for i in range(ends)])  6.74 us
    slice x4, local copies, waits for them, and re-layouts, with_halo(): head = lax.slice_in_dim(cells, 0, width, axis=dim)  5.35 us
    ppermute x3, starting transfers between devices, shifted(): return lax.ppermute(block, axis, route)  5.32 us
    ppermute x3, starting transfers between devices, shifted_2(): return lax.ppermute(shard, axis, pairs)  4.39 us
  transfers between devices with their start and end apart: 16, of which 4 were waited for; matrix products, arithmetic and copies ran while one was open for 27% of the time, Pallas kernels for 0%

commit v1 on v0

v1 whole, which is shorter than its diff:
```python
import functools

import jax
import jax.numpy as jnp
from jax import lax
from jax.experimental import pallas as pl
from jax.experimental.pallas import tpu as pltpu
from jax.sharding import PartitionSpec as P

MESH = pl.DeviceIdType.MESH
STEPS = 2
PAD = 8
CHUNK = 32
F32 = jnp.float32


def kernel(
    sizes,
    ash,
    face,
    air,
    ground,
    spread,
    category,
    vent_row,
    vent_col,
    vent_lev,
    amount,
    depth,
    share,
    settled,
    upward,
    dens_a,
    dens_b,
    vpad,
    coef,
    trans,
    lower_rad,
    sent_rad,
    col_send,
    col_recv,
    col_mix,
    row_send,
    row_recv,
    vent_amount,
    load_sem,
    send_sem,
    recv_sem,
    above_send,
    above_recv,
    rad_send,
    rad_recv,
):
    lon_n, lat_n = sizes
    grains, levels, rows, cols = ash.shape
    bands = depth.shape[0]
    vents = amount.shape[0]
    chunks = rows // CHUNK
    tiles = rows // 8
    lon = lax.axis_index("lon")
    lat = lax.axis_index("lat")
    lev = lax.axis_index("lev")
    is_south = lat == 0
    is_north = lat == lat_n - 1
    east_id = lax.rem(lon + 1, lon_n)
    west_id = lax.rem(lon + lon_n - 1, lon_n)
    partner = lax.rem(lon + lon_n // 2, lon_n)
    north_dev = {
        "lon": jnp.where(is_north, partner, lon),
        "lat": jnp.where(is_north, lat, lat + 1),
    }
    south_dev = {
        "lon": jnp.where(is_south, partner, lon),
        "lat": jnp.where(is_south, lat, lat - 1),
    }
    north_slot = jnp.where(is_north, 1, 0)
    south_slot = jnp.where(is_south, 0, 1)

    loads = []
    for l in range(levels):
        loads.append(
            pltpu.make_async_copy(
                ash.at[:, l], dens_a.at[pl.ds(grains * l, grains), pl.ds(PAD, rows)], load_sem.at[l]
            )
        )
    loads.append(
        pltpu.make_async_copy(face.at[1], vpad.at[:, pl.ds(PAD, rows)], load_sem.at[levels])
    )
    for copy in loads:
        copy.start()

    barrier = pltpu.get_barrier_semaphore()
    for dev in ({"lon": east_id}, {"lon": west_id}, north_dev, south_dev, {"lev": 1 - lev}):
        pl.semaphore_signal(barrier, inc=1, device_id=dev, device_id_type=MESH)

    ids = []
    for s in range(vents):
        r = vent_row[s] - lat * rows
        c = vent_col[s] - lon * cols
        k = vent_lev[s] - lev * levels
        inside = (r >= 0) & (r < rows) & (c >= 0) & (c < cols) & (k >= 0) & (k < levels)
        ids.append(jnp.where(inside, (k * rows + r) * cols + c, -1))
    for s in range(vents):
        for g in range(grains):
            total = amount[s, g]
            for o in range(vents):
                if o != s:
                    total = total + jnp.where(ids[o] == ids[s], amount[o, g], 0.0)
            vent_amount[s, g] = total

    lane = lax.broadcasted_iota(jnp.int32, (CHUNK, cols), 1)
    first_lane = lane == 0
    last_lane = lane == cols - 1
    lane8 = lax.broadcasted_iota(jnp.int32, (8, cols), 1)
    pair8 = lane8 // 2
    even8 = lax.rem(lane8, 2) == 0
    cell = lax.broadcasted_iota(jnp.int32, (CHUNK, cols), 0) * cols + lane

    @pl.when(lev == 1)
    def _():
        zero = jnp.zeros((rows, cols), F32)
        for g in range(grains):
            dens_a[levels * grains + g, pl.ds(PAD, rows), :] = zero
            dens_b[levels * grains + g, pl.ds(PAD, rows), :] = zero

    def pack(step, l, src):
        def turn(t, carry):
            p0, p1 = carry
            at = pl.ds(pl.multiple_of(PAD + 8 * t, 8), 8)
            for q in range(3):
                here = pair8 == 16 * q + t
                move = 32 * q + 2 * t + 1
                p0 = jnp.where(here, pltpu.roll(src[grains * l + 2 * q, at, :], move, 1), p0)
                p1 = jnp.where(here, pltpu.roll(src[grains * l + 2 * q + 1, at, :], move, 1), p1)
            if step == 0:
                here = pair8 == 48 + t
                u = face[0, l, pl.ds(pl.multiple_of(8 * t, 8), 8), :]
                p0 = jnp.where(here, pltpu.roll(u, 97 + 2 * t, 1), p0)
            return p0, p1

        zero = jnp.zeros((8, cols), F32)
        p0, p1 = lax.fori_loop(0, tiles, turn, (zero, zero), unroll=4)
        col_send[step, l, 0] = p0
        col_send[step, l, 1] = p1
        for g in range(grains):
            row_send[step, l, 0, g : g + 1, :] = src[grains * l + g, PAD : PAD + 1, :]
            row_send[step, l, 1, g : g + 1, :] = src[
                grains * l + g, PAD + rows - 1 : PAD + rows, :
            ]
        if step == 0:
            row_send[step, l, 1, grains : grains + 1, :] = vpad[
                l, PAD + rows - 1 : PAD + rows, :
            ]

    def edge_copies(step, l):
        def col(slot, dev):
            return pltpu.make_async_remote_copy(
                src_ref=col_send.at[step, l],
                dst_ref=col_recv.at[step, l, slot],
                send_sem=send_sem.at[step, l, slot],
                recv_sem=recv_sem.at[step, l, slot],
                device_id={"lon": dev},
                device_id_type=MESH,
            )

        def row(edge, slot, dev):
            return pltpu.make_async_remote_copy(
                src_ref=row_send.at[step, l, edge],
                dst_ref=row_recv.at[step, l, slot],
                send_sem=send_sem.at[step, l, 2 + edge],
                recv_sem=recv_sem.at[step, l, 2 + slot],
                device_id=dev,
                device_id_type=MESH,
            )

        return [
            col(0, east_id),
            col(1, west_id),
            row(0, south_slot, south_dev),
            row(1, north_slot, north_dev),
        ]

    def wait_edges(step, l, src):
        for slot in range(2):
            pltpu.make_async_remote_copy(
                src_ref=col_send.at[step, l],
                dst_ref=col_recv.at[step, l, slot],
                send_sem=send_sem.at[step, l, slot],
                recv_sem=recv_sem.at[step, l, slot],
                device_id={"lon": east_id},
                device_id_type=MESH,
            ).wait_recv()
            pltpu.make_async_remote_copy(
                src_ref=row_send.at[step, l, slot],
                dst_ref=row_recv.at[step, l, slot],
                send_sem=send_sem.at[step, l, 2 + slot],
                recv_sem=recv_sem.at[step, l, 2 + slot],
                device_id={"lon": east_id},
                device_id_type=MESH,
            ).wait_recv()
        for v in range(2):
            col_mix[step, l, v] = jnp.where(
                even8, col_recv[step, l, 0, v], col_recv[step, l, 1, v]
            )
        for g in range(grains):
            src[grains * l + g, PAD - 1 : PAD, :] = row_recv[step, l, 0, g : g + 1, :]
            src[grains * l + g, PAD + rows : PAD + rows + 1, :] = row_recv[
                step, l, 1, g : g + 1, :
            ]
        if step == 0:
            row = row_recv[step, l, 0, grains : grains + 1, :]
            vpad[l, PAD - 1 : PAD, :] = jnp.where(is_south, jnp.zeros_like(row), row)

    def halo_lanes(packed, slot, c):
        parts = []
        for j in range(CHUNK // 8):
            t = c * (CHUNK // 8) + j
            parts.append(pltpu.roll(packed, cols - (32 * (slot // 2) + 2 * t + 1), 1))
        return jnp.concatenate(parts, axis=0)

    def advance(step, l, c, src, store):
        base = pl.multiple_of(c * CHUNK, CHUNK)
        mid = pl.ds(PAD + base, CHUNK)
        mix = [col_mix[step, l, v] for v in range(2)]
        plain = pl.ds(base, CHUNK)
        if step == 0:
            ue = face[0, l, plain, :]
            uw = pltpu.roll(jnp.where(last_lane, halo_lanes(mix[0], 6, c), ue), 1, 1)
            vn = vpad[l, mid, :]
            vs = vpad[l, pl.ds(PAD - 1 + base, CHUNK), :]
            pe, pw = -jnp.minimum(ue, 0.0), jnp.maximum(uw, 0.0)
            pn, ps = -jnp.minimum(vn, 0.0), jnp.maximum(vs, 0.0)
            own = (
                1.0
                - jnp.maximum(ue, 0.0)
                + jnp.minimum(uw, 0.0)
                - jnp.maximum(vn, 0.0)
                + jnp.minimum(vs, 0.0)
            )
            for j, value in enumerate((pe, pw, pn, ps, own)):
                coef[l, j, plain, :] = value
        else:
            pe, pw, pn, ps, own = (coef[l, j, plain, :] for j in range(5))
        offset = (l * rows + base) * cols
        hits = [cell == ids[s] - offset for s in range(vents)]
        for g in range(grains):
            i = grains * l + g
            x = src[i, mid, :]
            south = src[i, pl.ds(PAD - 1 + base, CHUNK), :]
            north = src[i, pl.ds(PAD + 1 + base, CHUNK), :]
            above = src[i + grains, mid, :]
            edge = halo_lanes(mix[g % 2], g, c)
            west = pltpu.roll(jnp.where(last_lane, edge, x), 1, 1)
            east = pltpu.roll(jnp.where(first_lane, edge, x), cols - 1, 1)
            m = spread[g, lev * levels + l]
            f = 0.04 * (1.0 + category[g].astype(F32))
            new = (
                (own - (4.0 * m + f)) * x
                + (pe + m) * east
                + (pw + m) * west
                + (pn + m) * north
                + (ps + m) * south
                + f * above
            )
            erupt = jnp.zeros_like(new)
            for s in range(vents):
                erupt = jnp.where(hits[s], vent_amount[s, g], erupt)
            store(g, mid, plain, new + erupt)

    def above_copy(step, src):
        return pltpu.make_async_remote_copy(
            src_ref=src.at[pl.ds(0, grains), pl.ds(PAD, rows)],
            dst_ref=src.at[pl.ds(levels * grains, grains), pl.ds(PAD, rows)],
            send_sem=above_send.at[step],
            recv_sem=above_recv.at[step],
            device_id={"lev": 1 - lev},
            device_id_type=MESH,
        )

    def rad_copy(c):
        part = pl.ds(pl.multiple_of(c * CHUNK, CHUNK), CHUNK)
        return pltpu.make_async_remote_copy(
            src_ref=sent_rad.at[:, part],
            dst_ref=lower_rad.at[:, part],
            send_sem=rad_send.at[c],
            recv_sem=rad_recv.at[c],
            device_id={"lev": 1 - lev},
            device_id_type=MESH,
        )

    for copy in loads:
        copy.wait()

    @pl.when(is_north)
    def _():
        for l in range(levels):
            vpad[l, PAD + rows - 1 : PAD + rows, :] = jnp.zeros((1, cols), F32)

    pack(0, 0, dens_a)
    pl.semaphore_wait(barrier, 5)
    for copy in edge_copies(0, 0):
        copy.start()

    @pl.when(lev == 1)
    def _():
        above_copy(0, dens_a).start()

    pack(0, 1, dens_a)
    for copy in edge_copies(0, 1):
        copy.start()

    def loop(body):
        def turn(c, carry):
            body(c)
            return carry

        lax.fori_loop(0, chunks, turn, 0)

    for l in range(levels):
        wait_edges(0, l, dens_a)
        if l == levels - 1:

            @pl.when(lev == 0)
            def _():
                above_copy(0, dens_a).wait_recv()

        def store(g, mid, plain, value, l=l):
            dens_b[grains * l + g, mid, :] = value

        loop(lambda c: advance(0, l, c, dens_a, store))
        pack(1, l, dens_b)
        for copy in edge_copies(1, l):
            copy.start()
        if l == 0:

            @pl.when(lev == 1)
            def _():
                above_copy(1, dens_b).start()

    def fourth(value):
        ratio = value / 250.0
        squared = ratio * ratio
        return squared * squared

    def finish(c, below):
        plain = pl.ds(pl.multiple_of(c * CHUNK, CHUNK), CHUNK)
        warm = [fourth(air[l, plain, :]) for l in range(levels)]
        for b in range(bands):
            rad = below(b, plain)
            for l in range(levels):
                rad = warm[l] + trans[b, l, plain, :] * (rad - warm[l])
                upward[b, l, plain, :] = share[b] * rad
            sent_rad[b, plain, :] = rad

    for l in range(levels):
        wait_edges(1, l, dens_b)
        if l == levels - 1:

            @pl.when(lev == 0)
            def _():
                above_copy(1, dens_b).wait_recv()

        def store(g, mid, plain, value, l=l):
            settled[g, l, plain, :] = value

        def second(c, l=l):
            advance(1, l, c, dens_b, store)
            plain = pl.ds(pl.multiple_of(c * CHUNK, CHUNK), CHUNK)
            field = [settled[g, l, plain, :] for g in range(grains)]
            for b in range(bands):
                optical = depth[b, 0] * field[0]
                for g in range(1, grains):
                    optical = optical + depth[b, g] * field[g]
                trans[b, l, plain, :] = jnp.exp(-optical)
            if l == levels - 1:

                @pl.when(lev == 0)
                def _():
                    heat = fourth(ground[plain, :])
                    finish(c, lambda b, part: heat)
                    rad_copy(c).start()

        loop(second)

    @pl.when(lev == 1)
    def _():
        def last(c):
            rad_copy(c).wait_recv()
            finish(c, lambda b, part: lower_rad[b, part, :])

        loop(last)

    for step in range(STEPS):
        for l in range(levels):
            for copy in edge_copies(step, l):
                copy.wait_send()

    @pl.when(lev == 1)
    def _():
        above_copy(0, dens_a).wait_send()
        above_copy(1, dens_b).wait_send()

    @pl.when(lev == 0)
    def _():
        loop(lambda c: rad_copy(c).wait_send())


def per_device(sizes, *args):
    (ash, face, spread, category, vrow, vcol, vlev, amount, depth, share, air, ground) = args
    grains, levels, rows, cols = ash.shape
    bands = depth.shape[0]
    vmem = pl.BlockSpec(memory_space=pltpu.VMEM)
    smem = pl.BlockSpec(memory_space=pltpu.SMEM)
    slots = (levels + 1) * grains
    scratch = [
        pltpu.VMEM((slots, rows + 2 * PAD, cols), F32),
        pltpu.VMEM((slots, rows + 2 * PAD, cols), F32),
        pltpu.VMEM((levels, rows + 2 * PAD, cols), F32),
        pltpu.VMEM((levels, 5, rows, cols), F32),
        pltpu.VMEM((bands, levels, rows, cols), F32),
        pltpu.VMEM((bands, rows, cols), F32),
        pltpu.VMEM((bands, rows, cols), F32),
        pltpu.VMEM((STEPS, levels, 2, 8, cols), F32),
        pltpu.VMEM((STEPS, levels, 2, 2, 8, cols), F32),
        pltpu.VMEM((STEPS, levels, 2, 8, cols), F32),
        pltpu.VMEM((STEPS, levels, 2, 8, cols), F32),
        pltpu.VMEM((STEPS, levels, 2, 8, cols), F32),
        pltpu.SMEM(amount.shape, F32),
        pltpu.SemaphoreType.DMA((levels + 1,)),
        pltpu.SemaphoreType.DMA((STEPS, levels, 4)),
        pltpu.SemaphoreType.DMA((STEPS, levels, 4)),
        pltpu.SemaphoreType.DMA((STEPS,)),
        pltpu.SemaphoreType.DMA((STEPS,)),
        pltpu.SemaphoreType.DMA((rows // CHUNK,)),
        pltpu.SemaphoreType.DMA((rows // CHUNK,)),
    ]
    return pl.pallas_call(
        functools.partial(kernel, sizes),
        out_shape=(
            jax.ShapeDtypeStruct(ash.shape, F32),
            jax.ShapeDtypeStruct((bands, levels, rows, cols), F32),
        ),
        in_specs=[vmem] * 4 + [smem] * 8,
        out_specs=(vmem, vmem),
        scratch_shapes=scratch,
        compiler_params=pltpu.CompilerParams(
            collective_id=0, has_side_effects=True, vmem_limit_bytes=32 * 1024 * 1024
        ),
    )(ash, face, air, ground, spread, category, vrow, vcol, vlev, amount, depth, share)


def solution(mesh):
    sizes = (mesh.shape["lon"], mesh.shape["lat"])
    field = P("members", "lev", "lat", "lon")
    placed = (
        field,
        P(None, "lev", "lat", "lon"),
        P(),
        P(),
        P("members"),
        P("members"),
        P("members"),
        P("members", None),
        P(),
        P(),
        P("lev", "lat", "lon"),
        P("lat", "lon"),
    )
    return jax.shard_map(
        functools.partial(per_device, sizes),
        mesh=mesh,
        in_specs=placed,
        out_specs=(field, field),
        check_vma=False,
    )
```

time: 121 us -> 29 us (0.24)
  starting transfers between devices: 28.2 us -> 0 us
  other arithmetic: 24.1 us -> 0 us
  waiting for transfers between devices: 22.7 us -> 0 us
  local copies, waits for them, and re-layouts: 28.7 us -> 9.74 us
  Pallas kernels: 0 us -> 18.3 us
  between operations: 14.3 us -> 0.67 us
  matrix products: 2.28 us -> 0 us
    ppermute x14 -> x0, starting transfers between devices: 28.2 us -> none  [the longest x4 11.7 us: with_halo(): lax.ppermute(tail, axis, [(i, (i + 1) % count) for i in range(ends)])]
    all_gather x2 -> x0, waiting for transfers between devices: 19.2 us -> none  [prefix(): pieces = jax.tree.map(lambda part: lax.all_gather(part, axis), value)]
    pallas_call x0 -> x1, Pallas kernels: none -> 18.3 us  [per_device(): pl.pallas_call(functools.partial(kernel, sizes), out_shape=(jax.ShapeDtyp...]
    slice x10 -> x0, local copies, waits for them, and re-layouts: 9.68 us -> none  [the longest x4 5.35 us: with_halo(): head = lax.slice_in_dim(cells, 0, width, axis=dim)]
    add x6 -> x0, other arithmetic: 8.4 us -> none  [the longest x2 6.8 us: per_device(): update(density, east_cell, west_cell, north_cell, south_cell, above_cell,...]
    ppermute x4 -> x0, local copies, waits for them, and re-layouts: 6.12 us -> none  [the longest x2 3.4 us: with_halo(): lax.ppermute(head, axis, [((i + 1) % count, i) for i in range(ends)])]
    concatenate x2 -> x0, other arithmetic: 4.33 us -> none  [with_halo(): jnp.concatenate([lax.ppermute(tail, axis, [(i, (i + 1) % count) for i in...]
    mul x6 -> x0, other arithmetic: 3.25 us -> none  [the longest x1 1.23 us: per_device(): slab_trans = slab_trans * transmit]
  transfers between devices with their start and end apart: 16 -> 0, of which waited for: 4 -> 0; matrix products, arithmetic and copies ran while one was open for 27% -> 0% of each run, Pallas kernels for 0% -> 0%
where the time goes in v1:
time: 29 us; the launch traced here: 28.7 us
  Pallas kernels  18.3 us (63%)
  local copies, waits for them, and re-layouts  9.74 us (34%)
  between operations  0.67 us (2%)
    pallas_call x1, Pallas kernels, per_device(): pl.pallas_call(functools.partial(kernel, sizes), out_shape=(jax.ShapeDtyp...  18.3 us
    unnamed x25, local copies, waits for them, and re-layouts  9.74 us

profile of v1, /device:TPU:0, one launch (start us, length us, event | category | flops | bytes accessed | tf_op | source)
XLA Modules:
  0.0 28.7 jit_solution(1794441011388533889)
XLA Ops:
  0.6 0.0 copy-start.4
  0.6 0.0 copy-start.5
  0.7 0.8 %copy.14.spread = f32[6,4]{1,0:T(8,128)S(1)} copy(f32[6,4]{0,1:T(4,128)} %param.14) | data formatting | bytes 192 | tf_op args[2]
  1.4 0.0 copy-done.4
  1.4 0.0 copy-done.5
  1.4 0.0 copy-start
  1.4 1.1 %copy-done = f32[6,2,128,128]{3,2,1,0:T(8,128)S(1)} copy-done((f32[6,2,128,128]{3,2,1,0:T(8,128)S(1)}, f32[6,2,128,128]{3,2,1,0:T(8,128)}, u32[]{:S(2)}) %copy-start) | copy-done | bytes 786456
  2.6 0.0 copy-start.1
  2.6 0.9 %copy-done.1 = f32[2,2,128,128]{3,2,1,0:T(8,128)S(1)} copy-done((f32[2,2,128,128]{3,2,1,0:T(8,128)S(1)}, f32[2,2,128,128]{3,2,1,0:T(8,128)}, u32[]{:S(2)}) %copy-start.1) | copy-done | bytes 262168
  3.5 0.0 copy-start.2
  3.5 0.9 %copy-done.2 = f32[2,128,128]{2,1,0:T(8,128)S(1)} copy-done((f32[2,128,128]{2,1,0:T(8,128)S(1)}, f32[2,128,128]{2,1,0:T(8,128)}, u32[]{:S(2)}) %copy-start.2) | copy-done | bytes 131096
  4.4 0.8 %copy-done.3 = f32[128,128]{1,0:T(8,128)S(1)} copy-done((f32[128,128]{1,0:T(8,128)S(1)}, f32[128,128]{1,0:T(8,128)}, u32[]{:S(2)}) %copy-start.3) | copy-done | bytes 65560
  5.3 0.7 %copy-done.6 = s32[6]{0:T(128)S(1)} copy-done((s32[6]{0:T(128)S(1)}, s32[6]{0:T(128)}, u32[]{:S(2)}) %copy-start.6) | copy-done | bytes 48
  5.9 0.0 copy-start.7
  5.9 0.7 %copy-done.7 = s32[4]{0:T(128)S(1)} copy-done((s32[4]{0:T(128)S(1)}, s32[4]{0:T(128)}, u32[]{:S(2)}) %copy-start.7) | copy-done | bytes 40
  6.6 0.0 copy-start.8
  6.6 0.7 %copy-done.8 = s32[4]{0:T(128)S(1)} copy-done((s32[4]{0:T(128)S(1)}, s32[4]{0:T(128)}, u32[]{:S(2)}) %copy-start.8) | copy-done | bytes 40
  7.2 0.0 copy-start.9
  7.2 0.7 %copy-done.9 = s32[4]{0:T(128)S(1)} copy-done((s32[4]{0:T(128)S(1)}, s32[4]{0:T(128)}, u32[]{:S(2)}) %copy-start.9) | copy-done | bytes 40
  7.9 0.0 copy-start.10
  7.9 0.7 %copy-done.10 = f32[8]{0:T(128)S(1)} copy-done((f32[8]{0:T(128)S(1)}, f32[8]{0:T(128)}, u32[]{:S(2)}) %copy-start.10) | copy-done | bytes 56
  8.5 18.3 %shard_map.131 = (f32[6,2,128,128]{3,2,1,0:T(8,128)S(1)}, f32[8,2,128,128]{3,2,1,0:T(8,128)S(1)}) custom-call(f32[6,2,128,128]{3,2,1,0:T(8,128)S(1)} %copy-done, f32[2,2,128,128]{3,2,1,0:T(8,128)S(1)} %copy-done.1, f32[2,128,128]{2,1,0:T(8,128)S(1)} %copy-done.2, f32[128,128]{1,0:T(8,128)S(1)} %copy-done.3, f32[6,4]{1,0:T(8,128)S(1)} %copy.14.spread, ...), custom_call_target="tpu_custom_call" | custom-call | tf_op jit(solution)/shard_map/pallas_call | solution.py:437
  26.8 0.9 %copy.17 = f32[6,2,128,128]{3,2,1,0:T(8,128)} copy(f32[6,2,128,128]{3,2,1,0:T(8,128)S(1)} %get-tuple-element.4) | data formatting | bytes 1572864
  27.7 1.0 %copy.18 = f32[8,2,128,128]{3,2,1,0:T(8,128)} copy(f32[8,2,128,128]{3,2,1,0:T(8,128)S(1)} %get-tuple-element.5) | data formatting | bytes 2097152
  (2 shorter events, 0.0 us)
Async XLA Ops:
  0.6 0.8 %copy-start.4 = (f32[8,6]{1,0:T(8,128)S(1)}, f32[8,6]{1,0:T(8,128)}, u32[]{:S(2)}) copy-start(f32[8,6]{1,0:T(8,128)} %depth.1) | copy-start | bytes 580
  0.6 0.8 %copy-start.5 = (f32[4,6]{1,0:T(4,128)S(1)}, f32[4,6]{1,0:T(4,128)}, u32[]{:S(2)}) copy-start(f32[4,6]{1,0:T(4,128)} %amount.1) | copy-start | bytes 292
  1.4 1.1 %copy-start = (f32[6,2,128,128]{3,2,1,0:T(8,128)S(1)}, f32[6,2,128,128]{3,2,1,0:T(8,128)}, u32[]{:S(2)}) copy-start(f32[6,2,128,128]{3,2,1,0:T(8,128)} %ash.1) | copy-start | bytes 2359300
  2.6 0.9 %copy-start.1 = (f32[2,2,128,128]{3,2,1,0:T(8,128)S(1)}, f32[2,2,128,128]{3,2,1,0:T(8,128)}, u32[]{:S(2)}) copy-start(f32[2,2,128,128]{3,2,1,0:T(8,128)} %face.1) | copy-start | bytes 786436
  3.5 0.9 %copy-start.2 = (f32[2,128,128]{2,1,0:T(8,128)S(1)}, f32[2,128,128]{2,1,0:T(8,128)}, u32[]{:S(2)}) copy-start(f32[2,128,128]{2,1,0:T(8,128)} %air.1) | copy-start | bytes 393220
  4.4 0.8 %copy-start.3 = (f32[128,128]{1,0:T(8,128)S(1)}, f32[128,128]{1,0:T(8,128)}, u32[]{:S(2)}) copy-start(f32[128,128]{1,0:T(8,128)} %ground.1) | copy-start | bytes 196612
  5.3 0.7 %copy-start.6 = (s32[6]{0:T(128)S(1)}, s32[6]{0:T(128)}, u32[]{:S(2)}) copy-start(s32[6]{0:T(128)} %category.1) | copy-start | bytes 76
  5.9 0.7 %copy-start.7 = (s32[4]{0:T(128)S(1)}, s32[4]{0:T(128)}, u32[]{:S(2)}) copy-start(s32[4]{0:T(128)} %vent_row.1) | copy-start | bytes 52
  6.6 0.7 %copy-start.8 = (s32[4]{0:T(128)S(1)}, s32[4]{0:T(128)}, u32[]{:S(2)}) copy-start(s32[4]{0:T(128)} %vent_col.1) | copy-start | bytes 52
  7.2 0.7 %copy-start.9 = (s32[4]{0:T(128)S(1)}, s32[4]{0:T(128)}, u32[]{:S(2)}) copy-start(s32[4]{0:T(128)} %vent_lev.1) | copy-start | bytes 52
  7.9 0.7 %copy-start.10 = (f32[8]{0:T(128)S(1)}, f32[8]{0:T(128)}, u32[]{:S(2)}) copy-start(f32[8]{0:T(128)} %share.1) | copy-start | bytes 100

commit v2 on v1

--- a/solution.py
+++ b/solution.py
@@ -17,9 +17,23 @@
 def kernel(
     sizes,
     ash,
-    face,
-    air,
-    ground,
+    face_hbm,
+    air_hbm,
+    ground_hbm,
+    *rest,
+):
+    smalls, rest = rest[:8], rest[8:]
+    small_copies, rest = rest[-9:-1], rest[:-9] + rest[-1:]
+    body(sizes, ash, face_hbm, air_hbm, ground_hbm, smalls, *small_copies, *rest)
+
+
+def body(
+    sizes,
+    ash,
+    face_hbm,
+    air_hbm,
+    ground_hbm,
+    smalls,
     spread,
     category,
     vent_row,
@@ -30,6 +44,9 @@
     share,
     settled,
     upward,
+    face,
+    air,
+    ground,
     dens_a,
     dens_b,
     vpad,
@@ -50,6 +67,7 @@
     above_recv,
     rad_send,
     rad_recv,
+    small_sem,
 ):
     lon_n, lat_n = sizes
     grains, levels, rows, cols = ash.shape
@@ -84,14 +102,27 @@
             )
         )
     loads.append(
-        pltpu.make_async_copy(face.at[1], vpad.at[:, pl.ds(PAD, rows)], load_sem.at[levels])
+        pltpu.make_async_copy(face_hbm.at[1], vpad.at[:, pl.ds(PAD, rows)], load_sem.at[levels])
     )
-    for copy in loads:
+    loads.append(pltpu.make_async_copy(face_hbm.at[0], face, load_sem.at[levels + 1]))
+    late = [
+        pltpu.make_async_copy(air_hbm, air, load_sem.at[levels + 2]),
+        pltpu.make_async_copy(ground_hbm, ground, load_sem.at[levels + 3]),
+    ]
+    held = (spread, category, vent_row, vent_col, vent_lev, amount, depth, share)
+    little = [
+        pltpu.make_async_copy(source, target, small_sem.at[n])
+        for n, (source, target) in enumerate(zip(smalls, held))
+    ]
+    for copy in loads + little + late:
         copy.start()
 
     barrier = pltpu.get_barrier_semaphore()
     for dev in ({"lon": east_id}, {"lon": west_id}, north_dev, south_dev, {"lev": 1 - lev}):
         pl.semaphore_signal(barrier, inc=1, device_id=dev, device_id_type=MESH)
+
+    for copy in little:
+        copy.wait()
 
     ids = []
     for s in range(vents):
@@ -134,7 +165,7 @@
                 p1 = jnp.where(here, pltpu.roll(src[grains * l + 2 * q + 1, at, :], move, 1), p1)
             if step == 0:
                 here = pair8 == 48 + t
-                u = face[0, l, pl.ds(pl.multiple_of(8 * t, 8), 8), :]
+                u = face[l, pl.ds(pl.multiple_of(8 * t, 8), 8), :]
                 p0 = jnp.where(here, pltpu.roll(u, 97 + 2 * t, 1), p0)
             return p0, p1
 
@@ -224,7 +255,7 @@
         mix = [col_mix[step, l, v] for v in range(2)]
         plain = pl.ds(base, CHUNK)
         if step == 0:
-            ue = face[0, l, plain, :]
+            ue = face[l, plain, :]
             uw = pltpu.roll(jnp.where(last_lane, halo_lanes(mix[0], 6, c), ue), 1, 1)
             vn = vpad[l, mid, :]
             vs = vpad[l, pl.ds(PAD - 1 + base, CHUNK), :]
@@ -252,7 +283,7 @@
             edge = halo_lanes(mix[g % 2], g, c)
             west = pltpu.roll(jnp.where(last_lane, edge, x), 1, 1)
             east = pltpu.roll(jnp.where(first_lane, edge, x), cols - 1, 1)
-            m = spread[g, lev * levels + l]
+            m = spread[lev * levels + l, g]
             f = 0.04 * (1.0 + category[g].astype(F32))
             new = (
                 (own - (4.0 * m + f)) * x
@@ -352,6 +383,8 @@
                 upward[b, l, plain, :] = share[b] * rad
             sent_rad[b, plain, :] = rad
 
+    for copy in late:
+        copy.wait()
     for l in range(levels):
         wait_edges(1, l, dens_b)
         if l == levels - 1:
@@ -410,9 +443,11 @@
     grains, levels, rows, cols = ash.shape
     bands = depth.shape[0]
     vmem = pl.BlockSpec(memory_space=pltpu.VMEM)
-    smem = pl.BlockSpec(memory_space=pltpu.SMEM)
     slots = (levels + 1) * grains
     scratch = [
+        pltpu.VMEM((levels, rows, cols), F32),
+        pltpu.VMEM((levels, rows, cols), F32),
+        pltpu.VMEM((rows, cols), F32),
         pltpu.VMEM((slots, rows + 2 * PAD, cols), F32),
         pltpu.VMEM((slots, rows + 2 * PAD, cols), F32),
         pltpu.VMEM((levels, rows + 2 * PAD, cols), F32),
@@ -426,7 +461,7 @@
         pltpu.VMEM((STEPS, levels, 2, 8, cols), F32),
         pltpu.VMEM((STEPS, levels, 2, 8, cols), F32),
         pltpu.SMEM(amount.shape, F32),
-        pltpu.SemaphoreType.DMA((levels + 1,)),
+        pltpu.SemaphoreType.DMA((levels + 4,)),
         pltpu.SemaphoreType.DMA((STEPS, levels, 4)),
         pltpu.SemaphoreType.DMA((STEPS, levels, 4)),
         pltpu.SemaphoreType.DMA((STEPS,)),
@@ -434,19 +469,23 @@
         pltpu.SemaphoreType.DMA((rows // CHUNK,)),
         pltpu.SemaphoreType.DMA((rows // CHUNK,)),
     ]
+    smalls = (spread.T, category, vrow, vcol, vlev, amount, depth, share)
+    scratch += [pltpu.SMEM(small.shape, small.dtype) for small in smalls]
+    scratch.append(pltpu.SemaphoreType.DMA((len(smalls),)))
+    hbm = pl.BlockSpec(memory_space=pltpu.HBM)
     return pl.pallas_call(
         functools.partial(kernel, sizes),
         out_shape=(
             jax.ShapeDtypeStruct(ash.shape, F32),
             jax.ShapeDtypeStruct((bands, levels, rows, cols), F32),
         ),
-        in_specs=[vmem] * 4 + [smem] * 8,
+        in_specs=[hbm] * (4 + len(smalls)),
         out_specs=(vmem, vmem),
         scratch_shapes=scratch,
         compiler_params=pltpu.CompilerParams(
             collective_id=0, has_side_effects=True, vmem_limit_bytes=32 * 1024 * 1024
         ),
-    )(ash, face, air, ground, spread, category, vrow, vcol, vlev, amount, depth, share)
+    )(*[pltpu.with_memory_space_constraint(x, pltpu.HBM) for x in (ash, face, air, ground, *smalls)])
 
 
 def solution(mesh):

time: 29 us -> 20.1 us (0.69)
  local copies, waits for them, and re-layouts: 9.74 us -> 1.85 us
  Pallas kernels: 18.3 us -> 17.5 us
    unnamed x25 -> x2, local copies, waits for them, and re-layouts: 9.74 us -> 1.85 us
    pallas_call x1, Pallas kernels: 18.3 us -> 17.5 us  [per_device(): pl.pallas_call(functools.partial(kernel, sizes), out_shape=(jax.ShapeDtyp...]
where the time goes in v2:
time: 20.1 us; the launch traced here: 20 us
  Pallas kernels  17.5 us (87%)
  local copies, waits for them, and re-layouts  1.85 us (9%)
  between operations  0.64 us (3%)
    pallas_call x1, Pallas kernels, per_device(): pl.pallas_call(functools.partial(kernel, sizes), out_shape=(jax.ShapeDtyp...  17.5 us
    unnamed x2, local copies, waits for them, and re-layouts  1.85 us

profile of v2, /device:TPU:0, one launch (start us, length us, event | category | flops | bytes accessed | tf_op | source)
XLA Modules:
  0.0 20.0 jit_solution(14899533300175476317)
XLA Ops:
  0.6 17.5 %shard_map.131 = (f32[6,2,128,128]{3,2,1,0:T(8,128)S(1)}, f32[8,2,128,128]{3,2,1,0:T(8,128)S(1)}) custom-call(f32[6,2,128,128]{3,2,1,0:T(8,128)} %ash.1, f32[2,2,128,128]{3,2,1,0:T(8,128)} %face_hbm.1, f32[2,128,128]{2,1,0:T(8,128)} %air_hbm.1, f32[128,128]{1,0:T(8,128)} %ground_hbm.1, f32[4,6]{1,0:T(4,128)} %bitcast.1, s32[6]{0:T(128)} %rest_1_.1, ...), custom_call_target="tpu_custom_call" | custom-call | tf_op jit(solution)/shard_map/pallas_call | solution.py:476
  18.1 0.9 %copy.16 = f32[6,2,128,128]{3,2,1,0:T(8,128)} copy(f32[6,2,128,128]{3,2,1,0:T(8,128)S(1)} %get-tuple-element.4) | data formatting | bytes 1572864
  19.0 1.0 %copy.17 = f32[8,2,128,128]{3,2,1,0:T(8,128)} copy(f32[8,2,128,128]{3,2,1,0:T(8,128)S(1)} %get-tuple-element.5) | data formatting | bytes 2097152

commit v3 on v2

--- a/solution.py
+++ b/solution.py
@@ -94,6 +94,10 @@
     north_slot = jnp.where(is_north, 1, 0)
     south_slot = jnp.where(is_south, 0, 1)
 
+    barrier = pltpu.get_barrier_semaphore()
+    for dev in ({"lon": east_id}, {"lon": west_id}, north_dev, south_dev, {"lev": 1 - lev}):
+        pl.semaphore_signal(barrier, inc=1, device_id=dev, device_id_type=MESH)
+
     loads = []
     for l in range(levels):
         loads.append(
@@ -117,10 +121,6 @@
     for copy in loads + little + late:
         copy.start()
 
-    barrier = pltpu.get_barrier_semaphore()
-    for dev in ({"lon": east_id}, {"lon": west_id}, north_dev, south_dev, {"lev": 1 - lev}):
-        pl.semaphore_signal(barrier, inc=1, device_id=dev, device_id_type=MESH)
-
     for copy in little:
         copy.wait()
 
@@ -146,6 +146,14 @@
     pair8 = lane8 // 2
     even8 = lax.rem(lane8, 2) == 0
     cell = lax.broadcasted_iota(jnp.int32, (CHUNK, cols), 0) * cols + lane
+
+    no_row = jnp.zeros((1, cols), F32)
+    for l in range(levels):
+        vpad[l, PAD - 1 : PAD, :] = no_row
+        for g in range(grains):
+            for dens in (dens_a, dens_b):
+                dens[grains * l + g, PAD - 1 : PAD, :] = no_row
+                dens[grains * l + g, PAD + rows : PAD + rows + 1, :] = no_row
 
     @pl.when(lev == 1)
     def _():
@@ -211,7 +219,7 @@
             row(1, north_slot, north_dev),
         ]
 
-    def wait_edges(step, l, src):
+    def wait_edges(step, l):
         for slot in range(2):
             pltpu.make_async_remote_copy(
                 src_ref=col_send.at[step, l],
@@ -231,16 +239,10 @@
             ).wait_recv()
         for v in range(2):
             col_mix[step, l, v] = jnp.where(
-                even8, col_recv[step, l, 0, v], col_recv[step, l, 1, v]
-            )
-        for g in range(grains):
-            src[grains * l + g, PAD - 1 : PAD, :] = row_recv[step, l, 0, g : g + 1, :]
-            src[grains * l + g, PAD + rows : PAD + rows + 1, :] = row_recv[
-                step, l, 1, g : g + 1, :
-            ]
-        if step == 0:
-            row = row_recv[step, l, 0, grains : grains + 1, :]
-            vpad[l, PAD - 1 : PAD, :] = jnp.where(is_south, jnp.zeros_like(row), row)
+                even8,
+                pltpu.roll(col_recv[step, l, 1, v], cols - 1, 1),
+                pltpu.roll(col_recv[step, l, 0, v], 1, 1),
+            )
 
     def halo_lanes(packed, slot, c):
         parts = []
@@ -249,14 +251,50 @@
             parts.append(pltpu.roll(packed, cols - (32 * (slot // 2) + 2 * t + 1), 1))
         return jnp.concatenate(parts, axis=0)
 
+    def numbers(l, g):
+        return spread[lev * levels + l, g], 0.04 * (1.0 + category[g].astype(F32))
+
+    def fix_rows(step, l, src, out):
+        v_south = row_recv[0, l, 0, grains : grains + 1, :]
+        v_south = jnp.where(is_south, jnp.zeros_like(v_south), v_south)
+        to_south, from_own = jnp.maximum(v_south, 0.0), jnp.minimum(v_south, 0.0)
+        to_north = coef[l, 2, rows - 1 : rows, :]
+        for g in range(grains):
+            m, _ = numbers(l, g)
+            first, last = out(g, pl.ds(0, 1)), out(g, pl.ds(rows - 1, 1))
+            x = src[grains * l + g, PAD : PAD + 1, :]
+            ref, at = first
+            ref[at] = (
+                ref[at] + (to_south + m) * row_recv[step, l, 0, g : g + 1, :] + from_own * x
+            )
+            ref, at = last
+            ref[at] = ref[at] + (to_north + m) * row_recv[step, l, 1, g : g + 1, :]
+
+    def fix_cols(step, l, c, src, out):
+        base = pl.multiple_of(c * CHUNK, CHUNK)
+        mid = pl.ds(PAD + base, CHUNK)
+        plain = pl.ds(base, CHUNK)
+        u_west = halo_lanes(col_mix[0, l, 0], 6, c)
+        rate = jnp.where(first_lane, jnp.maximum(u_west, 0.0), coef[l, 0, plain, :])
+        from_own = jnp.where(first_lane, jnp.minimum(u_west, 0.0), 0.0)
+        ends = first_lane | last_lane
+        for g in range(grains):
+            m, f = numbers(l, g)
+            x = src[grains * l + g, mid, :]
+            edge = halo_lanes(col_mix[step, l, g % 2], g, c)
+            ref, at = out(g, plain)
+            new = ref[at] + jnp.where(ends, (rate + m) * edge + from_own * x, 0.0)
+            if l == levels - 1:
+                new = new + f * src[grains * levels + g, mid, :]
+            ref[at] = new
+
     def advance(step, l, c, src, store):
         base = pl.multiple_of(c * CHUNK, CHUNK)
         mid = pl.ds(PAD + base, CHUNK)
-        mix = [col_mix[step, l, v] for v in range(2)]
         plain = pl.ds(base, CHUNK)
         if step == 0:
             ue = face[l, plain, :]
-            uw = pltpu.roll(jnp.where(last_lane, halo_lanes(mix[0], 6, c), ue), 1, 1)
+            uw = jnp.where(first_lane, 0.0, pltpu.roll(ue, 1, 1))
             vn = vpad[l, mid, :]
             vs = vpad[l, pl.ds(PAD - 1 + base, CHUNK), :]
             pe, pw = -jnp.minimum(ue, 0.0), jnp.maximum(uw, 0.0)
@@ -279,20 +317,18 @@
             x = src[i, mid, :]
             south = src[i, pl.ds(PAD - 1 + base, CHUNK), :]
             north = src[i, pl.ds(PAD + 1 + base, CHUNK), :]
-            above = src[i + grains, mid, :]
-            edge = halo_lanes(mix[g % 2], g, c)
-            west = pltpu.roll(jnp.where(last_lane, edge, x), 1, 1)
-            east = pltpu.roll(jnp.where(first_lane, edge, x), cols - 1, 1)
-            m = spread[lev * levels + l, g]
-            f = 0.04 * (1.0 + category[g].astype(F32))
+            west = jnp.where(first_lane, 0.0, pltpu.roll(x, 1, 1))
+            east = jnp.where(last_lane, 0.0, pltpu.roll(x, cols - 1, 1))
+            m, f = numbers(l, g)
             new = (
                 (own - (4.0 * m + f)) * x
                 + (pe + m) * east
                 + (pw + m) * west
                 + (pn + m) * north
                 + (ps + m) * south
-                + f * above
-            )
+            )
+            if l < levels - 1:
+                new = new + f * src[i + grains, mid, :]
             erupt = jnp.zeros_like(new)
             for s in range(vents):
                 erupt = jnp.where(hits[s], vent_amount[s, g], erupt)
@@ -327,19 +363,6 @@
         for l in range(levels):
             vpad[l, PAD + rows - 1 : PAD + rows, :] = jnp.zeros((1, cols), F32)
 
-    pack(0, 0, dens_a)
-    pl.semaphore_wait(barrier, 5)
-    for copy in edge_copies(0, 0):
-        copy.start()
-
-    @pl.when(lev == 1)
-    def _():
-        above_copy(0, dens_a).start()
-
-    pack(0, 1, dens_a)
-    for copy in edge_copies(0, 1):
-        copy.start()
-
     def loop(body):
         def turn(c, carry):
             body(c)
@@ -347,18 +370,46 @@
 
         lax.fori_loop(0, chunks, turn, 0)
 
-    for l in range(levels):
-        wait_edges(0, l, dens_a)
+    def out_b(l):
+        def place(g, part):
+            shifted = pl.ds(part.start + PAD, part.size)
+            return dens_b, (grains * l + g, shifted, slice(None))
+
+        return place
+
+    def out_settled(l):
+        return lambda g, part: (settled, (g, l, part, slice(None)))
+
+    def run(step, l, src, out):
+        def store(g, mid, plain, value):
+            ref, at = out(g, plain)
+            ref[at] = value
+
+        loop(lambda c: advance(step, l, c, src, store))
+
+    for l in range(levels):
+        pack(0, l, dens_a)
+    for l in range(levels):
+        run(0, l, dens_a, out_b(l))
+    pl.semaphore_wait(barrier, 5)
+    for l in range(levels):
+        for copy in edge_copies(0, l):
+            copy.start()
+
+    @pl.when(lev == 1)
+    def _():
+        above_copy(0, dens_a).start()
+
+    for l in range(levels):
+        wait_edges(0, l)
         if l == levels - 1:
 
             @pl.when(lev == 0)
             def _():
                 above_copy(0, dens_a).wait_recv()
 
-        def store(g, mid, plain, value, l=l):
-            dens_b[grains * l + g, mid, :] = value
-
-        loop(lambda c: advance(0, l, c, dens_a, store))
+        fix_rows(0, l, dens_a, out_b(l))
+        loop(lambda c, l=l: fix_cols(0, l, c, dens_a, out_b(l)))
         pack(1, l, dens_b)
         for copy in edge_copies(1, l):
             copy.start()
@@ -386,18 +437,19 @@
     for copy in late:
         copy.wait()
     for l in range(levels):
-        wait_edges(1, l, dens_b)
+        run(1, l, dens_b, out_settled(l))
+    for l in range(levels):
+        wait_edges(1, l)
         if l == levels - 1:
 
             @pl.when(lev == 0)
             def _():
                 above_copy(1, dens_b).wait_recv()
 
-        def store(g, mid, plain, value, l=l):
-            settled[g, l, plain, :] = value
+        fix_rows(1, l, dens_b, out_settled(l))
 
         def second(c, l=l):
-            advance(1, l, c, dens_b, store)
+            fix_cols(1, l, c, dens_b, out_settled(l))
             plain = pl.ds(pl.multiple_of(c * CHUNK, CHUNK), CHUNK)
             field = [settled[g, l, plain, :] for g in range(grains)]
             for b in range(bands):
@@ -436,6 +488,17 @@
     @pl.when(lev == 0)
     def _():
         loop(lambda c: rad_copy(c).wait_send())
+
+
+def write_out(settled, upward, settled_out, upward_out, sem):
+    copies = [
+        pltpu.make_async_copy(settled, settled_out, sem.at[0]),
+        pltpu.make_async_copy(upward, upward_out, sem.at[1]),
+    ]
+    for copy in copies:
+        copy.start()
+    for copy in copies:
+        copy.wait()
 
 
 def per_device(sizes, *args):
@@ -473,11 +536,11 @@
     scratch += [pltpu.SMEM(small.shape, small.dtype) for small in smalls]
     scratch.append(pltpu.SemaphoreType.DMA((len(smalls),)))
     hbm = pl.BlockSpec(memory_space=pltpu.HBM)
-    return pl.pallas_call(
+    held = pl.pallas_call(
         functools.partial(kernel, sizes),
         out_shape=(
-            jax.ShapeDtypeStruct(ash.shape, F32),
-            jax.ShapeDtypeStruct((bands, levels, rows, cols), F32),
+            pltpu.VMEM(ash.shape, F32),
+            pltpu.VMEM((bands, levels, rows, cols), F32),
         ),
         in_specs=[hbm] * (4 + len(smalls)),
         out_specs=(vmem, vmem),
@@ -486,6 +549,13 @@
             collective_id=0, has_side_effects=True, vmem_limit_bytes=32 * 1024 * 1024
         ),
     )(*[pltpu.with_memory_space_constraint(x, pltpu.HBM) for x in (ash, face, air, ground, *smalls)])
+    return pl.pallas_call(
+        write_out,
+        out_shape=[jax.ShapeDtypeStruct(x.shape, F32) for x in held],
+        in_specs=[vmem] * 2,
+        out_specs=[pl.BlockSpec(memory_space=pl.ANY)] * 2,
+        scratch_shapes=[pltpu.SemaphoreType.DMA((2,))],
+    )(*[pltpu.with_memory_space_constraint(x, pltpu.VMEM) for x in held])
 
 
 def solution(mesh):

time: 20.1 us -> 19.1 us (0.950)
  local copies, waits for them, and re-layouts: 1.85 us -> 0 us
  Pallas kernels: 17.5 us -> 18.3 us
    unnamed x2 -> x0, local copies, waits for them, and re-layouts: 1.85 us -> none
    pallas_call x1 -> x2, Pallas kernels: 17.5 us -> 18.3 us  [the longest x1 17.1 us: per_device(): pl.pallas_call(functools.partial(kernel, sizes), out_shape=(pltpu.VMEM(as...]
where the time goes in v3:
time: 19.1 us; the launch traced here: 19 us
  Pallas kernels  18.3 us (96%)
  between operations  0.64 us (3%)
    pallas_call x1, Pallas kernels, per_device(): pl.pallas_call(functools.partial(kernel, sizes), out_shape=(pltpu.VMEM(as...  17.1 us
    pallas_call x1, Pallas kernels, per_device(): pl.pallas_call(write_out, out_shape=[jax.ShapeDtypeStruct(x.shape, F32) f...  1.25 us

profile of v3, /device:TPU:0, one launch (start us, length us, event | category | flops | bytes accessed | tf_op | source)
XLA Modules:
  0.0 19.0 jit_solution(12984523977083220443)
XLA Ops:
  0.6 17.1 %shard_map.131 = (f32[6,2,128,128]{3,2,1,0:T(8,128)S(1)}, f32[8,2,128,128]{3,2,1,0:T(8,128)S(1)}) custom-call(f32[6,2,128,128]{3,2,1,0:T(8,128)} %ash.1, f32[2,2,128,128]{3,2,1,0:T(8,128)} %face_hbm.1, f32[2,128,128]{2,1,0:T(8,128)} %air_hbm.1, f32[128,128]{1,0:T(8,128)} %ground_hbm.1, f32[4,6]{1,0:T(4,128)} %bitcast.1, s32[6]{0:T(128)} %rest_1_.1, ...), custom_call_target="tpu_custom_call" | custom-call | tf_op jit(solution)/shard_map/pallas_call | solution.py:539
  17.7 1.2 %shard_map.132 = (f32[6,2,128,128]{3,2,1,0:T(8,128)}, f32[8,2,128,128]{3,2,1,0:T(8,128)}) custom-call(f32[6,2,128,128]{3,2,1,0:T(8,128)S(1)} %get-tuple-element.4.settled, f32[8,2,128,128]{3,2,1,0:T(8,128)S(1)} %get-tuple-element.5.upward), custom_call_target="tpu_custom_call" | custom-call | tf_op jit(solution)/shard_map/pallas_call | solution.py:552

commit v4 on v3

--- a/solution.py
+++ b/solution.py
@@ -389,8 +389,6 @@
 
     for l in range(levels):
         pack(0, l, dens_a)
-    for l in range(levels):
-        run(0, l, dens_a, out_b(l))
     pl.semaphore_wait(barrier, 5)
     for l in range(levels):
         for copy in edge_copies(0, l):
@@ -400,6 +398,8 @@
     def _():
         above_copy(0, dens_a).start()
 
+    for l in range(levels):
+        run(0, l, dens_a, out_b(l))
     for l in range(levels):
         wait_edges(0, l)
         if l == levels - 1:

time: 19.1 us -> 18.5 us (0.969)
  Pallas kernels: 18.3 us -> 17.7 us
    pallas_call x1, Pallas kernels: 17.1 us -> 16.5 us  [per_device(): pl.pallas_call(functools.partial(kernel, sizes), out_shape=(pltpu.VMEM(as...]
where the time goes in v4:
time: 18.5 us; the launch traced here: 18.4 us
  Pallas kernels  17.7 us (96%)
  between operations  0.64 us (3%)
    pallas_call x1, Pallas kernels, per_device(): pl.pallas_call(functools.partial(kernel, sizes), out_shape=(pltpu.VMEM(as...  16.5 us
    pallas_call x1, Pallas kernels, per_device(): pl.pallas_call(write_out, out_shape=[jax.ShapeDtypeStruct(x.shape, F32) f...  1.25 us

profile of v4, /device:TPU:0, one launch (start us, length us, event | category | flops | bytes accessed | tf_op | source)
XLA Modules:
  0.0 18.4 jit_solution(11865547998689073458)
XLA Ops:
  0.6 16.5 %shard_map.131 = (f32[6,2,128,128]{3,2,1,0:T(8,128)S(1)}, f32[8,2,128,128]{3,2,1,0:T(8,128)S(1)}) custom-call(f32[6,2,128,128]{3,2,1,0:T(8,128)} %ash.1, f32[2,2,128,128]{3,2,1,0:T(8,128)} %face_hbm.1, f32[2,128,128]{2,1,0:T(8,128)} %air_hbm.1, f32[128,128]{1,0:T(8,128)} %ground_hbm.1, f32[4,6]{1,0:T(4,128)} %bitcast.1, s32[6]{0:T(128)} %rest_1_.1, ...), custom_call_target="tpu_custom_call" | custom-call | tf_op jit(solution)/shard_map/pallas_call | solution.py:539
  17.1 1.2 %shard_map.132 = (f32[6,2,128,128]{3,2,1,0:T(8,128)}, f32[8,2,128,128]{3,2,1,0:T(8,128)}) custom-call(f32[6,2,128,128]{3,2,1,0:T(8,128)S(1)} %get-tuple-element.4.settled, f32[8,2,128,128]{3,2,1,0:T(8,128)S(1)} %get-tuple-element.5.upward), custom_call_target="tpu_custom_call" | custom-call | tf_op jit(solution)/shard_map/pallas_call | solution.py:552
